TPU v7x, 512 devices: a whole 4x4x16 slice. The times are simulated.
512 devices in a mesh: day: 64 (over z, y), pair: 8 (over x, core).
Axes of the slice: x: 4, y: 4, z: 16, core: 2. Of those that a mesh axis runs over, the one named last changes fastest.
Arguments:
- spectra: bfloat16 [128, 128, 4096], P('day', 'pair'), may hold values from -40 to 40
- pair_stations: int32 [512, 2], P('pair'), may hold values from 0 to 127
- availability: int32 [128, 128], P('day'), may hold values from 0 to 1
Outputs:
- stacks: bfloat16 [128, 512, 1001], P('day', 'pair')
- reference: float32 [512, 1001], P('pair')
All inputs are finite; a program needn't handle non-finite values.
Results may differ from a plain program's by a relative error of at most 0.008.
Values may be sent and summed in bfloat16 or wider, within the bound.
A program may use at most 64 MiB of HBM per device.

v0:
```python
import jax
import jax.numpy as jnp
import numpy as np
from jax import lax
from jax.sharding import PartitionSpec as P

LAGS = 1001
WIDE = 1024
WINDOW = 30


def lag_table(bin_count):
    bin_ids = np.arange(bin_count)[:, None]
    lag_ids = np.arange(LAGS)[None, :] - (LAGS - 1) // 2
    angle = np.mod(bin_ids * lag_ids, 2 * bin_count) * (np.pi / bin_count)
    factor = 1.0 / np.sqrt(2.0 * bin_count)
    table = np.concatenate([np.cos(angle) * factor, -np.sin(angle) * factor], 0)
    return np.pad(table, ((0, 0), (0, WIDE - LAGS))).astype(np.float32).astype(jnp.bfloat16)


def per_device(spectra, pair_stations, availability):
    days_here = spectra.shape[0]
    groups = lax.axis_size("day")
    station_count = spectra.shape[1] * lax.axis_size("pair")
    bin_count = spectra.shape[2] // 2
    pairs_here = pair_stations.shape[0]
    inverse = jnp.asarray(lag_table(bin_count))
    station_ids = jnp.arange(station_count, dtype=jnp.int32)
    ends = jnp.concatenate([pair_stations[:, 0], pair_stations[:, 1]], 0)
    pick = (ends[:, None] == station_ids[None, :]).astype(jnp.bfloat16)
    avail = jnp.dot(availability.astype(jnp.bfloat16), pick.T, preferred_element_type=jnp.float32)
    present = avail[:, :pairs_here] * avail[:, pairs_here:]
    gathered = lax.all_gather(spectra, "pair", axis=1, tiled=True)
    rows = []
    for day in range(days_here):
        spec = jnp.dot(pick, gathered[day], preferred_element_type=jnp.float32)
        one, two = (spec[:pairs_here], spec[pairs_here:])
        ar, ai, br, bi = (
            one[:, :bin_count],
            one[:, bin_count:],
            two[:, :bin_count],
            two[:, bin_count:],
        )
        rows.append(jnp.concatenate([ar * br + ai * bi, ar * bi - ai * br], 1).astype(jnp.bfloat16))
    cross = jnp.concatenate(rows, 0)
    corr = jnp.dot(cross, inverse, preferred_element_type=jnp.float32)
    column = lax.broadcasted_iota(jnp.int32, (1, WIDE), 1)
    shown = present.reshape(-1, 1)
    daily = jnp.where(column == LAGS, shown, corr * shown).astype(jnp.bfloat16)
    daily = daily.reshape(days_here, pairs_here, WIDE)
    turned = lax.all_to_all(daily, "day", split_axis=1, concat_axis=0, tiled=True)
    days = groups * days_here
    mine = turned.reshape(days, WIDE)
    day_ids = np.arange(days)
    gap = day_ids[:, None] - day_ids[None, :]
    band = jnp.asarray(((gap >= 0) & (gap < WINDOW)).astype(np.float32), dtype=jnp.bfloat16)
    moving = jnp.dot(band, mine, preferred_element_type=jnp.float32)
    counts = moving[:, LAGS : LAGS + 1]
    ref = jnp.sum(mine.astype(jnp.float32), axis=0) / days
    ref = jnp.where(column[0] < LAGS, ref, 0.0)
    scale = jnp.sqrt(jnp.sum(ref * ref) / LAGS + 1e-06)
    stacks = (moving / jnp.maximum(counts, 1.0) / scale).astype(jnp.bfloat16)
    back = lax.all_to_all(
        stacks.reshape(days, 1, WIDE), "day", split_axis=0, concat_axis=1, tiled=True
    )
    ref_all = lax.all_gather(ref[None], "day", axis=0, tiled=True)
    return (back[:, :, :LAGS], ref_all[:, :LAGS])


def solution(mesh):
    return jax.shard_map(
        per_device,
        mesh=mesh,
        in_specs=(P("day", "pair", None), P("pair", None), P("day", None)),
        out_specs=(P("day", "pair", None), P("pair", None)),
        check_vma=False,
    )
```

profile of v0, /device:TPU:8, one launch (start us, length us, event | category | flops | bytes accessed | tf_op | source)
XLA Modules:
  0.0 198.5 jit_solution(13838983268094882941)
XLA Ops:
  7.2 0.0 all-gather.3.cloned.1.call-start
  7.2 0.7 all-gather.3.cloned.1.call-update
  7.9 0.8 slice_bitcast_fusion.5
  8.7 0.1 pad_add_fusion
  8.7 0.9 convolution_bitcast_fusion
  9.6 0.1 slice_multiply_fusion
  9.7 0.1 broadcast_in_dim.28
  9.8 37.6 %all-gather.3.cloned.1.call-done = bf16[2,128,4096]{2,1,0:T(8,128)(2,1)} async-done(((bf16[2,16,4096]{2,1,0:T(8,128)(2,1)}), bf16[2,128,4096]{2,1,0:T(8,128)(2,1)}) %all-gather.3.cloned.1.call-update) | async-done | bytes 2097168 | tf_op jit(solution)/shard_map/all_gather | solution.py:33
  47.4 1.8 fusion.3
  49.2 0.1 copy-done
  49.3 0.5 fusion.2
  49.8 0.4 add_convert_fusion
  50.2 2.5 %copy-done.2 = bf16[4096,1024]{1,0:T(8,128)(2,1)S(1)} copy-done((bf16[4096,1024]{1,0:T(8,128)(2,1)S(1)}, bf16[4096,1024]{1,0:T(8,128)(2,1)}, u32[]{:S(2)}) %copy-start.2) | copy-done | bytes 8388632
  52.7 1.3 fusion.1
  54.0 0.3 copy.12
  54.3 37.4 %all_to_all.33 = bf16[2,64,1024]{2,0,1:T(2,128)(2,1)S(1)} all-to-all(bf16[2,64,1024]{2,0,1:T(2,128)(2,1)S(1)} %copy.12), channel_id=1, replica_groups=mesh['day'=64,'pair'=8] {'day'}, dimensions={1} | all-to-all | bytes 524288 | tf_op jit(solution)/shard_map/all_to_all | solution.py:51
  91.7 0.2 convert_reduce_fusion
  91.9 0.6 broadcast_multiply_fusion
  93.3 0.2 fusion.18
  93.5 0.2 fusion.11
  93.7 0.1 fusion.9
  93.8 0.5 broadcast.36
  94.3 0.8 reduce.6
  95.1 0.8 reshape.58
  95.9 5.9 %all-to-all-start.1 = ((bf16[64,2,1024]{2,1,0:T(2,128)(2,1)}), bf16[64,2,1024]{2,1,0:T(2,128)(2,1)S(1)}, u32[]{:S(2)}, u32[]{:S(2)}) async-start(bf16[64,2,1024]{2,1,0:T(2,128)(2,1)} %reshape.58), calls=%async_computation.1 | async-start | bytes 524288 | tf_op jit(solution)/shard_map/all_to_all | solution.py:63
  101.9 86.4 %all-gather = f32[64,1,1024]{2,1,0:T(1,128)S(1)} all-gather(f32[1,1,1024]{2,1,0:T(1,128)S(1)} %fusion.15), channel_id=1, replica_groups=mesh['day'=64,'pair'=8] {'day'}, dimensions={0}, use_global_device_ids=true | all-gather | bytes 266240 | tf_op jit(solution)/shard_map/all_gather | solution.py:66
  188.3 0.8 copy.19
  189.1 0.0 all-to-all-done.1
  189.1 0.2 reshape.59
  189.3 1.5 reduce.4
  190.8 0.1 all_to_all.28
  190.9 0.8 copy.15
  (7 shorter events, 0.1 us)
Async XLA Ops:
  7.2 40.2 %all-gather.3.cloned.1.call-start = ((), (), s32[]{:S(2)}) async-start(), calls=%async_computation.2 | async-start | bytes 2359296 | tf_op jit(solution)/shard_map/all_gather | solution.py:33
  47.4 1.9 copy-start
  49.3 3.4 %copy-start.2 = (bf16[4096,1024]{1,0:T(8,128)(2,1)S(1)}, bf16[4096,1024]{1,0:T(8,128)(2,1)}, u32[]{:S(2)}) copy-start(bf16[4096,1024]{1,0:T(8,128)(2,1)} %constant.19.clone) | copy-start | bytes 25165828
  52.7 40.6 %copy-start.1 = (bf16[128,128]{1,0:T(8,128)(2,1)S(1)}, bf16[128,128]{1,0:T(8,128)(2,1)}, u32[]{:S(2)}) copy-start(bf16[128,128]{1,0:T(8,128)(2,1)} %constant.25) | copy-start | bytes 98308
  95.9 93.1 %all-to-all-start.1 = ((bf16[64,2,1024]{2,1,0:T(2,128)(2,1)}), bf16[64,2,1024]{2,1,0:T(2,128)(2,1)S(1)}, u32[]{:S(2)}, u32[]{:S(2)}) async-start(bf16[64,2,1024]{2,1,0:T(2,128)(2,1)} %reshape.58), calls=%async_computation.1 | async-start | bytes 524288 | tf_op jit(solution)/shard_map/all_to_all | solution.py:63
Sparse Core Ops, SparseCore 0:
  10.1 37.1 all-gather.2
where the time goes:
time: 199 us
  blocking collectives  124 us (62%)
  waiting for transfers between devices  38.3 us (19%)
  between operations  14.8 us (7%)
  local copies, waits for them, and re-layouts  6.83 us (3%)
  starting transfers between devices  5.97 us (3%)
  matrix products  4.73 us (2%)
  other arithmetic  4.04 us (2%)
    all_gather x1, blocking collectives, per_device(): ref_all = lax.all_gather(ref[None], 'day', axis=0, tiled=True)  86.4 us
    all_gather x1, waiting for transfers between devices, per_device(): gathered = lax.all_gather(spectra, 'pair', axis=1, tiled=True)  37.6 us
    all_to_all x1, blocking collectives, per_device(): lax.all_to_all(daily, 'day', split_axis=1, concat_axis=0, tiled=True)  37.4 us
    all_to_all x1, starting transfers between devices, per_device(): lax.all_to_all(stacks.reshape(days, 1, WIDE), 'day', split_axis=0, concat...  5.93 us
    unnamed x10, local copies, waits for them, and re-layouts  5.05 us
  transfers between devices with their start and end apart: 2, of which 1 were waited for; matrix products, arithmetic and copies ran while one was open for 1% of the time, Pallas kernels for 0%

commit v1 on v0

--- a/solution.py
+++ b/solution.py
@@ -63,7 +63,9 @@
     back = lax.all_to_all(
         stacks.reshape(days, 1, WIDE), "day", split_axis=0, concat_axis=1, tiled=True
     )
-    ref_all = lax.all_gather(ref[None], "day", axis=0, tiled=True)
+    ref_all = jnp.concatenate(
+        lax.all_to_all(jnp.stack(lax.axis_size("day") * [ref[None]]), "day", 0, 0), 0
+    )
     return (back[:, :, :LAGS], ref_all[:, :LAGS])
 
 

time: 199 us -> 158 us (0.79)
  blocking collectives: 124 us -> 64.4 us
  waiting for transfers between devices: 38.3 us -> 56.9 us
    all_gather x1 -> x0, blocking collectives: 86.4 us -> none  [per_device(): ref_all = lax.all_gather(ref[None], 'day', axis=0, tiled=True)]
    all_to_all x0 -> x1, blocking collectives: none -> 27 us  [per_device(): lax.all_to_all(stacks.reshape(days, 1, WIDE), 'day', split_axis=0, concat...]
    all_to_all x1, waiting for transfers between devices: 0.01 us -> 18.6 us  [per_device(): lax.all_to_all(jnp.stack(lax.axis_size('day') * [ref[None]]), 'day', 0, 0)]
  transfers between devices with their start and end apart: 2 -> 2, of which waited for: 1 -> 2; matrix products, arithmetic and copies ran while one was open for 1% -> 3% of each run, Pallas kernels for 0% -> 0%
where the time goes in v1:
time: 158 us; the launch traced here: 157 us
  blocking collectives  64.4 us (41%)
  waiting for transfers between devices  56.9 us (36%)
  between operations  14.8 us (9%)
  local copies, waits for them, and re-layouts  6.99 us (4%)
  starting transfers between devices  5.56 us (4%)
  matrix products  4.73 us (3%)
  other arithmetic  4.03 us (3%)
    all_gather x1, waiting for transfers between devices, per_device(): gathered = lax.all_gather(spectra, 'pair', axis=1, tiled=True)  37.6 us
    all_to_all x1, blocking collectives, per_device(): lax.all_to_all(daily, 'day', split_axis=1, concat_axis=0, tiled=True)  37.4 us
    all_to_all x1, blocking collectives, per_device(): lax.all_to_all(stacks.reshape(days, 1, WIDE), 'day', split_axis=0, concat...  27 us
    all_to_all x1, waiting for transfers between devices, per_device(): lax.all_to_all(jnp.stack(lax.axis_size('day') * [ref[None]]), 'day', 0, 0)  18.6 us
    all_to_all x1, starting transfers between devices, per_device(): lax.all_to_all(jnp.stack(lax.axis_size('day') * [ref[None]]), 'day', 0, 0)  5.52 us
    unnamed x10, local copies, waits for them, and re-layouts  4.37 us
  transfers between devices with their start and end apart: 2, of which 2 were waited for; matrix products, arithmetic and copies ran while one was open for 3% of the time, Pallas kernels for 0%

profile of v1, /device:TPU:8, one launch (start us, length us, event | category | flops | bytes accessed | tf_op | source)
XLA Modules:
  0.0 157.4 jit_solution(8390079436361872115)
XLA Ops:
  7.2 0.7 all-gather.2.cloned.1.call-update
  7.9 0.8 slice_bitcast_fusion.5
  8.7 0.1 pad_add_fusion
  8.7 0.9 convolution_bitcast_fusion
  9.6 0.1 slice_multiply_fusion
  9.7 0.1 broadcast_in_dim.25
  9.8 37.6 %all-gather.2.cloned.1.call-done = bf16[2,128,4096]{2,1,0:T(8,128)(2,1)} async-done(((bf16[2,16,4096]{2,1,0:T(8,128)(2,1)}), bf16[2,128,4096]{2,1,0:T(8,128)(2,1)}) %all-gather.2.cloned.1.call-update) | async-done | bytes 2097168 | tf_op jit(solution)/shard_map/all_gather | solution.py:33
  47.4 1.8 %fusion.3 = f32[128,4096]{1,0:T(8,128)S(1)} fusion(bf16[2,128,4096]{2,1,0:T(8,128)(2,1)} %all-gather.2.cloned.1.call-done, s32[128]{0:T(128)S(1)} %pad_add_fusion), kind=kOutput, calls=%fused_computation.7 | convolution fusion | flops 134234112 | bytes 3146240 | tf_op jit(solution)/shard_map/dot_general | solution.py:36
  49.2 0.1 copy-done
  49.3 0.5 fusion.2
  49.8 0.4 add_convert_fusion
  50.2 2.5 %copy-done.2 = bf16[4096,1024]{1,0:T(8,128)(2,1)S(1)} copy-done((bf16[4096,1024]{1,0:T(8,128)(2,1)S(1)}, bf16[4096,1024]{1,0:T(8,128)(2,1)}, u32[]{:S(2)}) %copy-start.2) | copy-done | bytes 8388632
  52.7 1.3 fusion.1
  54.0 0.3 copy.12
  54.3 37.4 %all_to_all.38 = bf16[2,64,1024]{2,0,1:T(2,128)(2,1)S(1)} all-to-all(bf16[2,64,1024]{2,0,1:T(2,128)(2,1)S(1)} %copy.12), channel_id=1, replica_groups=mesh['day'=64,'pair'=8] {'day'}, dimensions={1} | all-to-all | bytes 524288 | tf_op jit(solution)/shard_map/all_to_all | solution.py:51
  91.7 0.2 convert_reduce_fusion
  91.9 0.6 multiply_select_fusion
  93.3 0.2 fusion.17
  93.5 0.2 fusion.11
  93.7 0.1 fusion.9
  93.8 0.5 broadcast.30
  94.3 0.8 reduce.6
  95.1 0.1 reshape.53
  95.2 27.0 %all_to_all.39 = bf16[64,2,1024]{2,1,0:T(2,128)(2,1)S(1)} all-to-all(bf16[64,2,1024]{2,1,0:T(2,128)(2,1)S(1)} %reshape.53), channel_id=1, replica_groups=mesh['day'=64,'pair'=8] {'day'}, dimensions={0} | all-to-all | bytes 524288 | tf_op jit(solution)/shard_map/all_to_all | solution.py:63
  122.2 0.8 stack.3
  123.1 5.5 %all-to-all-start.2 = ((f32[64,1,1024]{2,1,0:T(1,128)}), f32[64,1,1024]{2,1,0:T(1,128)S(1)}, u32[]{:S(2)}, u32[]{:S(2)}) async-start(f32[64,1,1024]{2,1,0:T(1,128)} %stack.3), calls=%async_computation.2 | async-start | bytes 524288 | tf_op jit(solution)/shard_map/all_to_all | solution.py:67
  128.6 0.2 reshape.54
  128.9 1.5 reduce.4
  130.4 0.1 all_to_all.31
  130.5 0.8 copy.15
  131.2 18.6 %all-to-all-done.2 = f32[64,1,1024]{2,1,0:T(1,128)S(1)} async-done(((f32[64,1,1024]{2,1,0:T(1,128)}), f32[64,1,1024]{2,1,0:T(1,128)S(1)}, u32[]{:S(2)}, u32[]{:S(2)}) %all-to-all-start.2) | async-done | bytes 262176 | tf_op jit(solution)/shard_map/all_to_all | solution.py:67
  149.8 0.8 copy.19
  (7 shorter events, 0.1 us)
Async XLA Ops:
  7.2 40.2 %all-gather.2.cloned.1.call-start = ((), (), s32[]{:S(2)}) async-start(), calls=%async_computation.3 | async-start | bytes 2359296 | tf_op jit(solution)/shard_map/all_gather | solution.py:33
  47.4 1.9 %copy-start = (bf16[2,128,4096]{2,1,0:T(8,128)(2,1)S(1)}, bf16[2,128,4096]{2,1,0:T(8,128)(2,1)}, u32[]{:S(2)}) copy-start(bf16[2,128,4096]{2,1,0:T(8,128)(2,1)} %all-gather.2.cloned.1.call-done) | copy-start | bytes 6291460
  49.3 3.4 %copy-start.2 = (bf16[4096,1024]{1,0:T(8,128)(2,1)S(1)}, bf16[4096,1024]{1,0:T(8,128)(2,1)}, u32[]{:S(2)}) copy-start(bf16[4096,1024]{1,0:T(8,128)(2,1)} %constant.19.clone) | copy-start | bytes 25165828
  52.7 40.6 %copy-start.1 = (bf16[128,128]{1,0:T(8,128)(2,1)S(1)}, bf16[128,128]{1,0:T(8,128)(2,1)}, u32[]{:S(2)}) copy-start(bf16[128,128]{1,0:T(8,128)(2,1)} %constant.25) | copy-start | bytes 98308
  123.1 26.8 %all-to-all-start.2 = ((f32[64,1,1024]{2,1,0:T(1,128)}), f32[64,1,1024]{2,1,0:T(1,128)S(1)}, u32[]{:S(2)}, u32[]{:S(2)}) async-start(f32[64,1,1024]{2,1,0:T(1,128)} %stack.3), calls=%async_computation.2 | async-start | bytes 524288 | tf_op jit(solution)/shard_map/all_to_all | solution.py:67
Sparse Core Ops, SparseCore 0:
  10.1 37.1 all-gather.1
